TPU v7x, 32 devices: a whole 2x2x4 slice. The times are simulated.
32 devices in a mesh: dp: 4 (over z), label: 8 (over y, x, core).
Axes of the slice: x: 2, y: 2, z: 4, core: 2. Of those that a mesh axis runs over, the one named last changes fastest.
Arguments:
- queries: bfloat16 [4096, 1024], P(('dp', 'label')), may hold values from -6 to 6
- beams: int32 [4096, 20], P(('dp', 'label')), may hold values from 0 to 255, all different within a row; in each aligned block of 128 rows (0 to 127, 128 to 255, ...) at most 12 rows name the same one
- positive_slots: int32 [4096, 4], P(('dp', 'label')), may hold values from 0 to 2559
- owner: int32 [256], replicated, may hold values from 0 to 255, each once
- label_weight: bfloat16 [32768, 1024], P('label'), may hold values from -0.1875 to 0.1875
Outputs:
- query_grad: float32 [4096, 1024], P(('dp', 'label'))
- new_weight: float32 [32768, 1024], P(('label', 'dp'))
Inputs may be any that keep to these rules, and one draw needn't show every extreme that they name: `beams`: among the 128 rows of one device (aligned blocks of rows), no cluster is named by more than 12 rows, a bound that some block reaches; a row names 20 different clusters. `positive_slots`: position v stands for label v mod 128 of beam entry v // 128; repeats may occur. `owner`: each block of rows is named once.
All inputs are finite; a program needn't handle non-finite values.
Results may differ from a plain program's by a relative error of at most 0.0035.
Values may be sent and summed in bfloat16 or wider, within the bound.
A program may use at most 128 MiB of HBM per device.

v0:
```python
import functools

import jax
import jax.numpy as jnp
from jax import lax
from jax.experimental import pallas as pl
from jax.experimental.pallas import tpu as pltpu
from jax.sharding import PartitionSpec as P

STEP_SIZE = 0.02


def slot_table(keys, count, most):
    q_rows, beam = keys.shape
    pairs = q_rows * beam
    ids = jnp.arange(count, dtype=jnp.int32)
    member = jnp.any(keys[:, :, None] == ids[None, None, :], axis=1).astype(jnp.float32)
    row_ids = jnp.arange(q_rows, dtype=jnp.int32)
    lower = (row_ids[:, None] > row_ids[None, :]).astype(jnp.float32)
    before = jnp.dot(lower, member, precision=lax.Precision.HIGHEST)
    safe_keys = jnp.minimum(keys, count - 1)
    rank = jnp.take_along_axis(before, safe_keys, axis=1).astype(jnp.int32)
    flat_keys = keys.reshape(pairs)
    target = jnp.where(flat_keys < count, flat_keys * most + rank.reshape(pairs), count * most)
    table = (
        jnp.full((count * most,), pairs, jnp.int32)
        .at[target]
        .set(jnp.arange(pairs, dtype=jnp.int32), mode="drop")
    )
    return (target, table)


def body(queries, beams, positive_slots, owner, label_weight):
    n_label = lax.axis_size("label")
    q_dev, width = queries.shape
    beam = beams.shape[1]
    n_pos = positive_slots.shape[1]
    clusters = owner.shape[0]
    clus_dev = clusters // n_label
    cluster_size = label_weight.shape[0] // clus_dev
    most = max(2, q_dev * 3 // 32)
    pairs = q_dev * beam
    rows_dev = clus_dev * most
    lookup = beams[:, :, None] == jnp.arange(clusters, dtype=jnp.int32)[None, None, :]
    pair_slot = jnp.sum(jnp.where(lookup, owner[None, None, :], 0), axis=2)
    position = jnp.arange(beam, dtype=jnp.int32)
    inside = positive_slots[:, None, :] // cluster_size == position[None, :, None]
    pair_offset = jnp.where(inside, positive_slots[:, None, :] % cluster_size, -1)
    target, table = slot_table(pair_slot, clusters, most)
    filled = table < pairs
    padded = jnp.concatenate([queries, jnp.zeros((1, width), queries.dtype)], axis=0)
    send_q = padded[jnp.where(filled, table // beam, q_dev)]
    flat_off = pair_offset.reshape(pairs, n_pos)
    send_off = jnp.where(filled[:, None], flat_off[jnp.where(filled, table, 0)], -1)
    moved = (
        lax.all_to_all(
            send_q.reshape(n_label, rows_dev, width),
            "label",
            split_axis=0,
            concat_axis=0,
            tiled=True,
        ),
        lax.all_to_all(
            send_off.astype(jnp.bfloat16).reshape(n_label, rows_dev, n_pos),
            "label",
            split_axis=0,
            concat_axis=0,
            tiled=True,
        ),
        lax.all_to_all(
            filled.astype(jnp.bfloat16).reshape(n_label, rows_dev),
            "label",
            split_axis=0,
            concat_axis=0,
            tiled=True,
        ),
    )
    recv_q = moved[0]
    recv_off = moved[1].astype(jnp.int32)
    recv_fill = moved[2].astype(jnp.float32)
    incoming = n_label * most
    recv_q = (
        recv_q.reshape(n_label, clus_dev, most, width)
        .transpose(1, 0, 2, 3)
        .reshape(clus_dev, incoming, width)
    )
    recv_off = (
        recv_off.reshape(n_label, clus_dev, most, n_pos)
        .transpose(1, 0, 2, 3)
        .reshape(clus_dev, incoming, n_pos)
    )
    recv_fill = (
        recv_fill.reshape(n_label, clus_dev, most).transpose(1, 0, 2).reshape(clus_dev, incoming)
    )
    weights = label_weight.reshape(clus_dev, cluster_size, width)
    scores = jnp.einsum("cnd,cld->cnl", recv_q, weights, preferred_element_type=jnp.float32)
    labels = jnp.arange(cluster_size, dtype=jnp.int32)
    positive = jnp.any(recv_off[..., None] == labels, axis=-2).astype(jnp.float32)
    signal = ((jax.nn.sigmoid(scores) - positive) * recv_fill[..., None]).astype(jnp.bfloat16)
    signal_split = signal.reshape(clus_dev, n_label, most, cluster_size)
    part_dq = jnp.einsum(
        "csml,cld->scmd", signal_split, weights, preferred_element_type=jnp.float32
    ).astype(jnp.bfloat16)
    part_dw = jnp.einsum("cnl,cnd->cld", signal, recv_q, preferred_element_type=jnp.float32)
    part_dw = part_dw.reshape(clus_dev * cluster_size, width)
    back = lax.all_to_all(
        part_dq.reshape(n_label, rows_dev, width), "label", split_axis=0, concat_axis=0, tiled=True
    )
    back_rows = back.reshape(clusters * most, width)[target]
    query_grad = jnp.sum(back_rows.reshape(q_dev, beam, width).astype(jnp.float32), axis=1)
    summed = lax.psum_scatter(part_dw, "dp", scatter_dimension=0, tiled=True)
    share = summed.shape[0]
    own_rows = lax.dynamic_slice_in_dim(
        label_weight, lax.axis_index("dp") * share, share, 0
    ).astype(jnp.float32)
    return (query_grad, own_rows - STEP_SIZE * summed)


SLOTS = 16
CHUNK = 8


def tn_dot(a, b):
    return lax.dot_general(a, b, (((0,), (0,)), ((), ())), preferred_element_type=jnp.float32)


def nt_dot(a, b):
    return lax.dot_general(a, b, (((1,), (1,)), ((), ())), preferred_element_type=jnp.float32)


def pick_matrix(meta, beam, first):
    q_dev = meta.shape[1]
    ids = (first + lax.broadcasted_iota(jnp.int32, (CHUNK, q_dev), 0)).astype(jnp.float32)
    member = meta[32:33, :] == ids
    for j in range(1, beam):
        member = member | (meta[32 + j:33 + j, :] == ids)
    member = member.astype(jnp.float32)
    row = lax.broadcasted_iota(jnp.int32, (q_dev, q_dev), 0)
    col = lax.broadcasted_iota(jnp.int32, (q_dev, q_dev), 1)
    upper = (row < col).astype(jnp.float32).astype(jnp.bfloat16)
    rank = jnp.dot(member.astype(jnp.bfloat16), upper, preferred_element_type=jnp.float32)
    code = jnp.where(member > 0, rank, -1.0)
    wide = jnp.broadcast_to(code[:, None, :], (CHUNK, SLOTS, q_dev))
    place = lax.broadcasted_iota(jnp.int32, (CHUNK, SLOTS, q_dev), 1).astype(jnp.float32)
    pick = (wide == place).astype(jnp.float32).reshape(CHUNK * SLOTS, q_dev)
    return pick.astype(jnp.bfloat16)


def gather_chunk(blk_ref, src, b, first, at, beam, x_ref, off_ref):
    q_dev = blk_ref.shape[2]
    tiles = (blk_ref.shape[1] - 64) // q_dev
    meta = blk_ref[src, tiles * q_dev:tiles * q_dev + 64, :]
    pick = pick_matrix(meta.astype(jnp.float32), beam, first)
    q = jnp.concatenate([blk_ref[src, k * q_dev:(k + 1) * q_dev, :] for k in range(tiles)], axis=1)
    rows = jnp.dot(pick, q, preferred_element_type=jnp.float32).astype(jnp.bfloat16)
    here = pl.ds(pl.multiple_of(b * SLOTS, SLOTS), SLOTS)
    x_ref[pl.ds(at, CHUNK), here, :] = rows.reshape(CHUNK, SLOTS, rows.shape[1])
    high = nt_dot(pick, meta[0:16, :])
    low = nt_dot(pick, meta[16:32, :])
    cluster = first + lax.broadcasted_iota(jnp.int32, high.shape, 0) // SLOTS
    off = jnp.where(high == cluster.astype(jnp.float32), low, -1.0)
    off_ref[pl.ds(at, CHUNK), here, :] = off.reshape(CHUNK, SLOTS, 16)
    return pick


def signal_of(x, off, w, n_pos):
    score = nt_dot(x, w)
    label = lax.broadcasted_iota(jnp.int32, score.shape, 1).astype(jnp.float32)
    hit = off[:, 0:1] == label
    for p in range(1, n_pos):
        hit = hit | (off[:, p:p + 1] == label)
    return (jax.nn.sigmoid(score) - hit.astype(jnp.float32)).astype(jnp.bfloat16)


def step_kernel(n_dp, n_label, beam, n_pos, blk_ref, w_ref, part_ref, new_ref,
                x_ref, y_ref, pick_ref, off_ref, sig_ref):
    d, l = lax.axis_index("dp"), lax.axis_index("label")
    clus_dev = w_ref.shape[0]
    chunks = clus_dev // CHUNK
    rows = CHUNK * SLOTS

    @pl.loop(0, n_label)
    def _(b):
        for h in range(chunks):
            pick = gather_chunk(
                blk_ref, d * n_label + b, b, l * clus_dev + h * CHUNK, h * CHUNK, beam, x_ref, off_ref
            )
            pick_ref[b, h * rows:(h + 1) * rows, :] = pick

    @pl.loop(0, clus_dev // 2)
    def _(c2):
        for u in range(2):
            c = c2 * 2 + u
            w = w_ref[c]
            sig = signal_of(x_ref[c], off_ref[c], w, n_pos)
            sig_ref[c] = sig
            y_ref[c] = jnp.dot(sig, w, preferred_element_type=jnp.float32).astype(jnp.bfloat16)

    @pl.loop(0, n_label)
    def _(b):
        here = pl.ds(pl.multiple_of(b * SLOTS, SLOTS), SLOTS)
        y = y_ref[:, here, :].reshape(clus_dev * SLOTS, y_ref.shape[2])
        part_ref[b] = tn_dot(pick_ref[b], y).astype(jnp.bfloat16)

    @pl.loop(0, CHUNK)
    def _(c):
        at = d * CHUNK + c
        new_ref[c] = w_ref[at].astype(jnp.float32) - STEP_SIZE * tn_dot(sig_ref[at], x_ref[at])

    for step in range(1, n_dp):
        other = lax.rem(d + step, n_dp)

        @pl.loop(0, n_label)
        def _(b):
            gather_chunk(
                blk_ref, other * n_label + b, b, l * clus_dev + d * CHUNK, 0, beam, x_ref, off_ref
            )

        @pl.loop(0, CHUNK // 2)
        def _(c2):
            for u in range(2):
                c = c2 * 2 + u
                x = x_ref[c]
                sig = signal_of(x, off_ref[c], w_ref[d * CHUNK + c], n_pos)
                new_ref[c] = new_ref[c] - STEP_SIZE * tn_dot(sig, x)


def make_block(queries, beams, positive_slots, owner, cluster_size):
    q_dev, width = queries.shape
    beam, n_pos = beams.shape[1], positive_slots.shape[1]
    ids = jnp.arange(owner.shape[0], dtype=jnp.int32)
    lookup = beams[:, :, None] == ids[None, None, :]
    slot = jnp.sum(jnp.where(lookup, owner[None, None, :], 0), axis=2)
    where_p = positive_slots[:, :, None] // cluster_size == jnp.arange(beam, dtype=jnp.int32)
    pos_slot = jnp.sum(jnp.where(where_p, slot[:, None, :], 0), axis=2)
    pos_label = positive_slots % cluster_size
    meta = jnp.concatenate(
        [
            jnp.pad(pos_slot, ((0, 0), (0, 16 - n_pos))),
            jnp.pad(pos_label, ((0, 0), (0, 16 - n_pos))),
            jnp.pad(slot, ((0, 0), (0, 32 - beam)), constant_values=-1),
        ],
        axis=1,
    )
    tiles = queries.reshape(q_dev, width // q_dev, q_dev).transpose(1, 0, 2).reshape(width, q_dev)
    return jnp.concatenate([tiles, meta.T.astype(jnp.bfloat16)], axis=0)


def sparse_body(queries, beams, positive_slots, owner, label_weight):
    n_label = lax.axis_size("label")
    n_dp = lax.axis_size("dp")
    q_dev, width = queries.shape
    clus_dev = owner.shape[0] // n_label
    cluster_size = label_weight.shape[0] // clus_dev
    block = make_block(queries, beams, positive_slots, owner, cluster_size)
    blocks = lax.all_gather(block, ("dp", "label"), axis=0, tiled=False)
    slots = n_label * SLOTS
    part, new = pl.pallas_call(
        functools.partial(step_kernel, n_dp, n_label, beams.shape[1], positive_slots.shape[1]),
        out_shape=(
            jax.ShapeDtypeStruct((n_label, q_dev, width), jnp.bfloat16),
            jax.ShapeDtypeStruct((CHUNK, cluster_size, width), jnp.float32),
        ),
        in_specs=[pl.BlockSpec(memory_space=pltpu.VMEM)] * 2,
        out_specs=(pl.BlockSpec(memory_space=pltpu.VMEM),) * 2,
        scratch_shapes=[
            pltpu.VMEM((clus_dev, slots, width), jnp.bfloat16),
            pltpu.VMEM((clus_dev, slots, width), jnp.bfloat16),
            pltpu.VMEM((n_label, clus_dev * SLOTS, q_dev), jnp.bfloat16),
            pltpu.VMEM((clus_dev, slots, 16), jnp.float32),
            pltpu.VMEM((clus_dev, slots, cluster_size), jnp.bfloat16),
        ],
        compiler_params=pltpu.CompilerParams(vmem_limit_bytes=56 << 20),
    )(blocks, label_weight.reshape(clus_dev, cluster_size, width))
    back = lax.all_to_all(part, "label", split_axis=0, concat_axis=0, tiled=True)
    query_grad = jnp.sum(back.astype(jnp.float32), axis=0)
    return (query_grad, new.reshape(CHUNK * cluster_size, width))


def choose(queries, beams, positive_slots, owner, label_weight):
    n_dp, n_label = lax.axis_size("dp"), lax.axis_size("label")
    q_dev, width = queries.shape
    fits = queries.size * n_dp * n_label * 2 <= (8 << 20) and n_label * SLOTS == q_dev
    fits = fits and q_dev == 128 and width % q_dev == 0 and beams.shape[1] <= 32
    fits = fits and owner.shape[0] == n_label * n_dp * CHUNK and positive_slots.shape[1] <= 16
    fits = fits and max(2, q_dev * 3 // 32) <= SLOTS and owner.shape[0] <= 256
    form = sparse_body if fits else body
    return form(queries, beams, positive_slots, owner, label_weight)


def solution(mesh):
    in_specs = (
        P(("dp", "label"), None),
        P(("dp", "label"), None),
        P(("dp", "label"), None),
        P(),
        P("label", None),
    )
    out_specs = (P(("dp", "label"), None), P(("label", "dp"), None))
    return jax.shard_map(
        choose, mesh=mesh, in_specs=in_specs, out_specs=out_specs, check_vma=False
    )
```

profile of v0, /device:TPU:0, one launch (start us, length us, event | category | flops | bytes accessed | tf_op | source)
XLA Modules:
  0.0 187.4 jit_solution(3662016154187624615)
XLA Ops:
  7.2 0.0 all-gather.3.cloned.1.call-start
  7.2 0.7 add_select_fusion.1
  7.9 1.6 select_reduce_fusion
  9.6 1.0 copy.12
  10.7 0.7 pad_maximum_fusion
  11.4 0.0 all-gather.3.cloned.1.call-update
  11.4 82.5 %all-gather.3.cloned.1.call-done = bf16[34816,128]{1,0:T(8,128)(2,1)} async-done(((bf16[1088,128]{1,0:T(8,128)(2,1)}), bf16[34816,128]{1,0:T(8,128)(2,1)}) %all-gather.3.cloned.1.call-update) | async-done | bytes 8912912 | tf_op jit(solution)/shard_map/all_gather | solution.py:256
  93.9 55.4 %shard_map.68 = (bf16[8,128,1024]{2,1,0:T(8,128)(2,1)}, f32[8,128,1024]{2,1,0:T(8,128)}) custom-call(bf16[32,1088,128]{2,1,0:T(8,128)(2,1)} %bitcast.10, bf16[32,128,1024]{2,1,0:T(8,128)(2,1)} %bitcast.11), custom_call_target="tpu_custom_call" | custom-call | tf_op jit(solution)/shard_map/pallas_call | solution.py:258
  149.3 30.1 %all_to_all.5 = bf16[8,128,1024]{2,1,0:T(8,128)(2,1)S(1)} all-to-all(bf16[8,128,1024]{2,1,0:T(8,128)(2,1)} %get-tuple-element.4), channel_id=1, replica_groups=mesh['dp'=4,'label'=8] {'label'}, dimensions={0} | all-to-all | bytes 4194304 | tf_op jit(solution)/shard_map/all_to_all | solution.py:275
  179.4 1.1 convert_reduce_fusion
  (5 shorter events, 0.1 us)
Async XLA Ops:
  7.2 86.7 %all-gather.3.cloned.1.call-start = ((), (), s32[]{:S(2)}) async-start(), calls=%async_computation.1 | async-start | bytes 9191424 | tf_op jit(solution)/shard_map/all_gather | solution.py:256
Sparse Core Ops, SparseCore 0:
  11.5 82.3 all-gather.2
where the time goes:
time: 188 us; the launch traced here: 187 us
  waiting for transfers between devices  82.5 us (44%)
  Pallas kernels  55.4 us (29%)
  blocking collectives  30.1 us (16%)
  between operations  14.1 us (8%)
  other arithmetic  4.25 us (2%)
    all_gather x1, waiting for transfers between devices, sparse_body(): blocks = lax.all_gather(block, ('dp', 'label'), axis=0, tiled=False)  82.5 us
    pallas_call x1, Pallas kernels, sparse_body(): pl.pallas_call(functools.partial(step_kernel, n_dp, n_label, beams.shape[...  55.4 us
    all_to_all x1, blocking collectives, sparse_body(): lax.all_to_all(part, 'label', split_axis=0, concat_axis=0, tiled=True)  30.1 us
  transfers between devices with their start and end apart: 1, of which 1 were waited for; matrix products, arithmetic and copies ran while one was open for 0% of the time, Pallas kernels for 0%

commit v1 on v0

--- a/solution.py
+++ b/solution.py
@@ -116,6 +116,7 @@
     return (query_grad, own_rows - STEP_SIZE * summed)
 
 
+MESH = pl.DeviceIdType.MESH
 SLOTS = 16
 CHUNK = 8
 
@@ -172,49 +173,168 @@
     return (jax.nn.sigmoid(score) - hit.astype(jnp.float32)).astype(jnp.bfloat16)
 
 
-def step_kernel(n_dp, n_label, beam, n_pos, blk_ref, w_ref, part_ref, new_ref,
-                x_ref, y_ref, pick_ref, off_ref, sig_ref):
+def flip(l, j):
+    return ((l // 4 + j // 4) % 2) * 4 + ((l // 2 + j // 2) % 2) * 2 + (l + j) % 2
+
+
+def step_kernel(n_dp, n_label, beam, n_pos, mine_ref, w_hbm, grad_ref, new_ref,
+                blk_ref, w_ref, x_ref, y_ref, pick_ref, off_ref, sig_ref, part_ref, back_ref,
+                local_sem, recv_sem, half_sem, z_sem, send_sem, back_send, back_recv):
     d, l = lax.axis_index("dp"), lax.axis_index("label")
     clus_dev = w_ref.shape[0]
     chunks = clus_dev // CHUNK
     rows = CHUNK * SLOTS
-
-    @pl.loop(0, n_label)
-    def _(b):
-        for h in range(chunks):
-            pick = gather_chunk(
-                blk_ref, d * n_label + b, b, l * clus_dev + h * CHUNK, h * CHUNK, beam, x_ref, off_ref
-            )
-            pick_ref[b, h * rows:(h + 1) * rows, :] = pick
-
-    @pl.loop(0, clus_dev // 2)
-    def _(c2):
-        for u in range(2):
-            c = c2 * 2 + u
-            w = w_ref[c]
-            sig = signal_of(x_ref[c], off_ref[c], w, n_pos)
-            sig_ref[c] = sig
-            y_ref[c] = jnp.dot(sig, w, preferred_element_type=jnp.float32).astype(jnp.bfloat16)
-
-    @pl.loop(0, n_label)
-    def _(b):
-        here = pl.ds(pl.multiple_of(b * SLOTS, SLOTS), SLOTS)
-        y = y_ref[:, here, :].reshape(clus_dev * SLOTS, y_ref.shape[2])
-        part_ref[b] = tn_dot(pick_ref[b], y).astype(jnp.bfloat16)
+    length = blk_ref.shape[1]
+    half = length // 2
+    xn, yn, sib, diag = flip(l, 2), flip(l, 4), flip(l, 1), flip(l, 6)
+    whole, first, second = pl.ds(0, length), pl.ds(0, half), pl.ds(half, half)
+    near = jnp.where(d == 0, 1, jnp.where(d == 1, 0, jnp.where(d == 2, 3, 2)))
+    mid = jnp.where(d == 0, 2, jnp.where(d == 1, 2, 1))
+    far = jnp.where(d < 2, 3, 0)
+    planes = [d, near, mid, far]
+
+    load_w = pltpu.make_async_copy(w_hbm, w_ref, local_sem.at[0])
+    load_w.start()
+    load_q = pltpu.make_async_copy(mine_ref, blk_ref.at[d * n_label + l], local_sem.at[1])
+    load_q.start()
+
+    barrier = pltpu.get_barrier_semaphore()
+    for j in range(1, n_label):
+        pl.semaphore_signal(barrier, inc=1, device_id=(d, flip(l, j)), device_id_type=MESH)
+    for p in planes[1:]:
+        pl.semaphore_signal(barrier, inc=1, device_id=(p, l), device_id_type=MESH)
+    pl.semaphore_wait(barrier, n_label - 1 + n_dp - 1)
+
+    def copy(g, part, send, recv, to):
+        return pltpu.make_async_remote_copy(
+            src_ref=blk_ref.at[g, part], dst_ref=blk_ref.at[g, part], send_sem=send,
+            recv_sem=recv, device_id=to, device_id_type=MESH,
+        )
+
+    def z_copy(s):
+        g = d * n_label + l
+        return copy(g, whole, z_sem.at[s - 1], recv_sem.at[g], (planes[s], l))
+
+    def arrived(g, part, sem):
+        copy(g, part, z_sem.at[0], sem, (d, sib)).wait_recv()
+
+    def sends(s):
+        base = planes[s] * n_label
+        own, gx, gy, gd = base + l, base + xn, base + yn, base + diag
+        sem = [send_sem.at[s * 8 + i] for i in range(8)]
+        return [
+            (own, whole, sem[0], recv_sem.at[own], (d, xn)),
+            (own, whole, sem[1], recv_sem.at[own], (d, yn)),
+            (own, whole, sem[2], recv_sem.at[own], (d, sib)),
+            (gx, first, sem[3], recv_sem.at[gx], (d, yn)),
+            (gx, whole, sem[4], recv_sem.at[gx], (d, sib)),
+            (gy, second, sem[5], half_sem.at[planes[s]], (d, xn)),
+            (gy, whole, sem[6], recv_sem.at[gy], (d, sib)),
+            (gd, whole, sem[7], recv_sem.at[gd], (d, sib)),
+        ]
+
+    def stage_a(s):
+        g = planes[s] * n_label + l
+        if s > 0:
+            arrived(g, whole, recv_sem.at[g])
+        for c in sends(s)[:3]:
+            copy(*c).start()
+
+    def stage_b(s):
+        gx, gy = planes[s] * n_label + xn, planes[s] * n_label + yn
+        arrived(gx, whole, recv_sem.at[gx])
+        for c in sends(s)[3:5]:
+            copy(*c).start()
+        arrived(gy, whole, recv_sem.at[gy])
+        for c in sends(s)[5:7]:
+            copy(*c).start()
+
+    def stage_c(s):
+        g = planes[s] * n_label + diag
+        arrived(g, first, recv_sem.at[g])
+        arrived(g, second, half_sem.at[planes[s]])
+        copy(*sends(s)[7]).start()
+
+    def stage_d(s):
+        for j in (1, 3, 5, 7):
+            g = planes[s] * n_label + flip(l, j)
+            arrived(g, whole, recv_sem.at[g])
+
+    def gather_own(start, stop, stride):
+        @pl.loop(0, (stop - start + stride - 1) // stride)
+        def _(i):
+            j = start + i * stride
+            for h in range(chunks):
+                pick = gather_chunk(
+                    blk_ref, d * n_label + flip(l, j), j, l * clus_dev + h * CHUNK, h * CHUNK,
+                    beam, x_ref, off_ref,
+                )
+                pick_ref[j, h * rows:(h + 1) * rows, :] = pick
+
+    def signals(start, stop):
+        @pl.loop(start // 2, stop // 2)
+        def _(c2):
+            for u in range(2):
+                c = c2 * 2 + u
+                w = w_ref[c]
+                sig = signal_of(x_ref[c], off_ref[c], w, n_pos)
+                sig_ref[c] = sig
+                y_ref[c] = jnp.dot(sig, w, preferred_element_type=jnp.float32).astype(jnp.bfloat16)
+
+    def grad_copy(j):
+        return pltpu.make_async_remote_copy(
+            src_ref=part_ref.at[j], dst_ref=back_ref.at[j], send_sem=back_send.at[j],
+            recv_sem=back_recv.at[j], device_id=(d, flip(l, j)), device_id_type=MESH,
+        )
+
+    def part_of(j):
+        y = y_ref[:, j * SLOTS:(j + 1) * SLOTS, :].reshape(clus_dev * SLOTS, y_ref.shape[2])
+        return tn_dot(pick_ref[j], y)
+
+    load_q.wait()
+    stage_a(0)
+    for s in range(1, n_dp):
+        z_copy(s).start()
+    gather_own(0, 1, 1)
+    stage_b(0)
+    gather_own(2, 5, 2)
+    stage_c(0)
+    stage_a(1)
+    gather_own(6, 7, 1)
+    stage_d(0)
+    stage_b(1)
+    gather_own(1, 8, 2)
+    stage_c(1)
+    stage_a(2)
+    load_w.wait()
+    signals(0, clus_dev // 2)
+    stage_b(2)
+    stage_a(3)
+    signals(clus_dev // 2, clus_dev)
+    stage_c(2)
+    stage_b(3)
+    for j in (7, 6, 5, 3, 4, 2, 1):
+        part_ref[j] = part_of(j).astype(jnp.bfloat16)
+        grad_copy(j).start()
+    stage_c(3)
+    grad_ref[...] = part_of(0)
 
     @pl.loop(0, CHUNK)
     def _(c):
         at = d * CHUNK + c
         new_ref[c] = w_ref[at].astype(jnp.float32) - STEP_SIZE * tn_dot(sig_ref[at], x_ref[at])
 
-    for step in range(1, n_dp):
-        other = lax.rem(d + step, n_dp)
-
-        @pl.loop(0, n_label)
-        def _(b):
-            gather_chunk(
-                blk_ref, other * n_label + b, b, l * clus_dev + d * CHUNK, 0, beam, x_ref, off_ref
-            )
+    for s in range(1, n_dp):
+        stage_d(s)
+
+        @pl.loop(0, n_label // 2)
+        def _(i):
+            for u in range(2):
+                j = i * 2 + u
+                gather_chunk(
+                    blk_ref, planes[s] * n_label + j, j, l * clus_dev + d * CHUNK, 0, beam,
+                    x_ref, off_ref,
+                )
 
         @pl.loop(0, CHUNK // 2)
         def _(c2):
@@ -223,6 +343,20 @@
                 x = x_ref[c]
                 sig = signal_of(x, off_ref[c], w_ref[d * CHUNK + c], n_pos)
                 new_ref[c] = new_ref[c] - STEP_SIZE * tn_dot(sig, x)
+
+    for j in range(1, n_label):
+        grad_copy(j).wait_recv()
+    total = grad_ref[...]
+    for j in range(1, n_label):
+        total = total + back_ref[j].astype(jnp.float32)
+    grad_ref[...] = total
+    for j in range(1, n_label):
+        grad_copy(j).wait_send()
+    for s in range(1, n_dp):
+        z_copy(s).wait_send()
+    for s in range(n_dp):
+        for c in sends(s):
+            copy(*c).wait_send()
 
 
 def make_block(queries, beams, positive_slots, owner, cluster_size):
@@ -253,34 +387,45 @@
     clus_dev = owner.shape[0] // n_label
     cluster_size = label_weight.shape[0] // clus_dev
     block = make_block(queries, beams, positive_slots, owner, cluster_size)
-    blocks = lax.all_gather(block, ("dp", "label"), axis=0, tiled=False)
     slots = n_label * SLOTS
-    part, new = pl.pallas_call(
+    length = block.shape[0]
+    grad, new = pl.pallas_call(
         functools.partial(step_kernel, n_dp, n_label, beams.shape[1], positive_slots.shape[1]),
         out_shape=(
-            jax.ShapeDtypeStruct((n_label, q_dev, width), jnp.bfloat16),
+            jax.ShapeDtypeStruct((q_dev, width), jnp.float32),
             jax.ShapeDtypeStruct((CHUNK, cluster_size, width), jnp.float32),
         ),
-        in_specs=[pl.BlockSpec(memory_space=pltpu.VMEM)] * 2,
+        in_specs=[pl.BlockSpec(memory_space=pl.ANY)] * 2,
         out_specs=(pl.BlockSpec(memory_space=pltpu.VMEM),) * 2,
         scratch_shapes=[
+            pltpu.VMEM((n_dp * n_label, length, q_dev), jnp.bfloat16),
+            pltpu.VMEM((clus_dev, cluster_size, width), jnp.bfloat16),
             pltpu.VMEM((clus_dev, slots, width), jnp.bfloat16),
             pltpu.VMEM((clus_dev, slots, width), jnp.bfloat16),
             pltpu.VMEM((n_label, clus_dev * SLOTS, q_dev), jnp.bfloat16),
             pltpu.VMEM((clus_dev, slots, 16), jnp.float32),
             pltpu.VMEM((clus_dev, slots, cluster_size), jnp.bfloat16),
+            pltpu.VMEM((n_label, q_dev, width), jnp.bfloat16),
+            pltpu.VMEM((n_label, q_dev, width), jnp.bfloat16),
+            pltpu.SemaphoreType.DMA((2,)),
+            pltpu.SemaphoreType.DMA((n_dp * n_label,)),
+            pltpu.SemaphoreType.DMA((n_dp,)),
+            pltpu.SemaphoreType.DMA((n_dp - 1,)),
+            pltpu.SemaphoreType.DMA((8 * n_dp,)),
+            pltpu.SemaphoreType.DMA((n_label,)),
+            pltpu.SemaphoreType.DMA((n_label,)),
         ],
-        compiler_params=pltpu.CompilerParams(vmem_limit_bytes=56 << 20),
-    )(blocks, label_weight.reshape(clus_dev, cluster_size, width))
-    back = lax.all_to_all(part, "label", split_axis=0, concat_axis=0, tiled=True)
-    query_grad = jnp.sum(back.astype(jnp.float32), axis=0)
-    return (query_grad, new.reshape(CHUNK * cluster_size, width))
+        compiler_params=pltpu.CompilerParams(
+            vmem_limit_bytes=58 << 20, collective_id=0, has_side_effects=True
+        ),
+    )(block, label_weight.reshape(clus_dev, cluster_size, width))
+    return (grad, new.reshape(CHUNK * cluster_size, width))
 
 
 def choose(queries, beams, positive_slots, owner, label_weight):
     n_dp, n_label = lax.axis_size("dp"), lax.axis_size("label")
     q_dev, width = queries.shape
-    fits = queries.size * n_dp * n_label * 2 <= (8 << 20) and n_label * SLOTS == q_dev
+    fits = n_dp == 4 and n_label == 8 and queries.size * n_dp * n_label * 2 <= (8 << 20) and n_label * SLOTS == q_dev
     fits = fits and q_dev == 128 and width % q_dev == 0 and beams.shape[1] <= 32
     fits = fits and owner.shape[0] == n_label * n_dp * CHUNK and positive_slots.shape[1] <= 16
     fits = fits and max(2, q_dev * 3 // 32) <= SLOTS and owner.shape[0] <= 256

time: 188 us -> 101 us (0.54)
  waiting for transfers between devices: 82.5 us -> 0 us
  Pallas kernels: 55.4 us -> 89.9 us
  blocking collectives: 30.1 us -> 0 us
  between operations: 14.1 us -> 0.69 us
  local copies, waits for them, and re-layouts: 1.03 us -> 6.73 us
    all_gather x1 -> x0, waiting for transfers between devices: 82.5 us -> none  [sparse_body(): blocks = lax.all_gather(block, ('dp', 'label'), axis=0, tiled=False)]
    pallas_call x1, Pallas kernels: 55.4 us -> 89.9 us  [sparse_body(): pl.pallas_call(functools.partial(step_kernel, n_dp, n_label, beams.shape[...]
    all_to_all x1 -> x0, blocking collectives: 30.1 us -> none  [sparse_body(): lax.all_to_all(part, 'label', split_axis=0, concat_axis=0, tiled=True)]
    unnamed x1 -> x4, local copies, waits for them, and re-layouts: 0.99 us -> 6.68 us
  transfers between devices with their start and end apart: 1 -> 0, of which waited for: 1 -> 0; matrix products, arithmetic and copies ran while one was open for 0% -> 0% of each run, Pallas kernels for 0% -> 0%
where the time goes in v1:
time: 101 us; the launch traced here: 100 us
  Pallas kernels  89.9 us (89%)
  local copies, waits for them, and re-layouts  6.73 us (7%)
  other arithmetic  3.14 us (3%)
    pallas_call x1, Pallas kernels, sparse_body(): pl.pallas_call(functools.partial(step_kernel, n_dp, n_label, beams.shape[...  89.9 us
    unnamed x4, local copies, waits for them, and re-layouts  6.68 us

profile of v1, /device:TPU:0, one launch (start us, length us, event | category | flops | bytes accessed | tf_op | source)
XLA Modules:
  0.0 100.5 jit_solution(869298110327978318)
XLA Ops:
  0.6 0.0 copy-start
  0.6 0.7 add_select_fusion.1
  1.4 1.6 %select_reduce_fusion = s32[128,20]{0,1:T(8,128)S(1)} fusion(s32[256]{0:T(256)} %param.8, s32[128,20]{0,1:T(8,128)} %param.6), kind=kLoop, calls=%fused_computation | loop fusion | flops 1963520 | bytes 21504 | tf_op jit(solution)/shard_map/reduce_sum | solution.py:367
  3.1 0.0 copy-done
  3.1 0.7 pad_maximum_fusion.mine_ref
  3.9 89.9 %shard_map.68 = (f32[128,1024]{1,0:T(8,128)}, f32[8,128,1024]{2,1,0:T(8,128)}) custom-call(bf16[1088,128]{1,0:T(8,128)(2,1)} %pad_maximum_fusion.mine_ref, bf16[32,128,1024]{2,1,0:T(8,128)(2,1)} %bitcast.12), custom_call_target="tpu_custom_call" | custom-call | tf_op jit(solution)/shard_map/pallas_call | solution.py:392
  93.8 1.9 %copy.16 = f32[128,1024]{1,0:T(8,128)} copy(f32[128,1024]{1,0:T(8,128)} %get-tuple-element.10) | data formatting | bytes 1048576
  95.7 4.8 %copy.17 = f32[1024,1024]{1,0:T(8,128)} copy(f32[1024,1024]{1,0:T(8,128)} %bitcast.13) | data formatting | bytes 8388608
  (5 shorter events, 0.1 us)
Async XLA Ops:
  0.6 2.5 %copy-start = (bf16[128,1024]{1,0:T(8,128)(2,1)S(1)}, bf16[128,1024]{1,0:T(8,128)(2,1)}, u32[]{:S(2)}) copy-start(bf16[128,1024]{1,0:T(8,128)(2,1)} %param.5) | copy-start | bytes 786436

commit v2 on v1

--- a/solution.py
+++ b/solution.py
@@ -192,6 +192,9 @@
     mid = jnp.where(d == 0, 2, jnp.where(d == 1, 2, 1))
     far = jnp.where(d < 2, 3, 0)
     planes = [d, near, mid, far]
+    inner = (d == 1) | (d == 2)
+    toward = jnp.where(d < 2, d + 1, d - 1)
+    outward = jnp.where(d == 1, 0, 3)
 
     load_w = pltpu.make_async_copy(w_hbm, w_ref, local_sem.at[0])
     load_w.start()
@@ -212,8 +215,14 @@
         )
 
     def z_copy(s):
+        g = planes[s] * n_label + l
+        onward = jnp.where(planes[s] < d, d + 1, d - 1)
+        to = outward if s == 0 else jnp.minimum(onward, n_dp - 1)
+        return copy(g, whole, z_sem.at[s], recv_sem.at[g], (to, l))
+
+    def z_first():
         g = d * n_label + l
-        return copy(g, whole, z_sem.at[s - 1], recv_sem.at[g], (planes[s], l))
+        return copy(g, whole, z_sem.at[n_dp], recv_sem.at[g], (toward, l))
 
     def arrived(g, part, sem):
         copy(g, part, z_sem.at[0], sem, (d, sib)).wait_recv()
@@ -237,6 +246,13 @@
         g = planes[s] * n_label + l
         if s > 0:
             arrived(g, whole, recv_sem.at[g])
+        else:
+            z_first().start()
+
+        @pl.when(inner)
+        def _():
+            z_copy(s).start()
+
         for c in sends(s)[:3]:
             copy(*c).start()
 
@@ -282,42 +298,53 @@
                 y_ref[c] = jnp.dot(sig, w, preferred_element_type=jnp.float32).astype(jnp.bfloat16)
 
     def grad_copy(j):
+        slot = (j - 1) // 2 if j % 2 else 4 + j // 2
+        to = sib if j % 2 else flip(l, j)
         return pltpu.make_async_remote_copy(
-            src_ref=part_ref.at[j], dst_ref=back_ref.at[j], send_sem=back_send.at[j],
-            recv_sem=back_recv.at[j], device_id=(d, flip(l, j)), device_id_type=MESH,
+            src_ref=part_ref.at[j], dst_ref=back_ref.at[slot], send_sem=back_send.at[j],
+            recv_sem=back_recv.at[slot], device_id=(d, to), device_id_type=MESH,
         )
 
     def part_of(j):
         y = y_ref[:, j * SLOTS:(j + 1) * SLOTS, :].reshape(clus_dev * SLOTS, y_ref.shape[2])
         return tn_dot(pick_ref[j], y)
 
+    quarter = clus_dev // 4
     load_q.wait()
     stage_a(0)
-    for s in range(1, n_dp):
-        z_copy(s).start()
     gather_own(0, 1, 1)
     stage_b(0)
+    stage_a(1)
     gather_own(2, 5, 2)
     stage_c(0)
-    stage_a(1)
+    stage_a(2)
     gather_own(6, 7, 1)
     stage_d(0)
     stage_b(1)
-    gather_own(1, 8, 2)
+    gather_own(1, 4, 2)
+    stage_a(3)
     stage_c(1)
-    stage_a(2)
+    gather_own(5, 8, 2)
+    stage_b(2)
     load_w.wait()
-    signals(0, clus_dev // 2)
-    stage_b(2)
-    stage_a(3)
-    signals(clus_dev // 2, clus_dev)
+    signals(0, quarter)
     stage_c(2)
     stage_b(3)
-    for j in (7, 6, 5, 3, 4, 2, 1):
+    signals(quarter, 2 * quarter)
+    stage_c(3)
+    signals(2 * quarter, clus_dev)
+    for j in (7, 3, 5, 1):
         part_ref[j] = part_of(j).astype(jnp.bfloat16)
         grad_copy(j).start()
-    stage_c(3)
-    grad_ref[...] = part_of(0)
+    for j in (6, 2, 4, 0):
+        value = part_of(j)
+        grad_copy(j + 1).wait_recv()
+        value = value + back_ref[j // 2].astype(jnp.float32)
+        if j:
+            part_ref[j] = value.astype(jnp.bfloat16)
+            grad_copy(j).start()
+        else:
+            grad_ref[...] = value
 
     @pl.loop(0, CHUNK)
     def _(c):
@@ -344,16 +371,20 @@
                 sig = signal_of(x, off_ref[c], w_ref[d * CHUNK + c], n_pos)
                 new_ref[c] = new_ref[c] - STEP_SIZE * tn_dot(sig, x)
 
-    for j in range(1, n_label):
+    total = grad_ref[...]
+    for j in (2, 4, 6):
         grad_copy(j).wait_recv()
-    total = grad_ref[...]
-    for j in range(1, n_label):
-        total = total + back_ref[j].astype(jnp.float32)
+        total = total + back_ref[4 + j // 2].astype(jnp.float32)
     grad_ref[...] = total
     for j in range(1, n_label):
         grad_copy(j).wait_send()
-    for s in range(1, n_dp):
-        z_copy(s).wait_send()
+    z_first().wait_send()
+
+    @pl.when(inner)
+    def _():
+        for s in range(n_dp):
+            z_copy(s).wait_send()
+
     for s in range(n_dp):
         for c in sends(s):
             copy(*c).wait_send()
@@ -410,7 +441,7 @@
             pltpu.SemaphoreType.DMA((2,)),
             pltpu.SemaphoreType.DMA((n_dp * n_label,)),
             pltpu.SemaphoreType.DMA((n_dp,)),
-            pltpu.SemaphoreType.DMA((n_dp - 1,)),
+            pltpu.SemaphoreType.DMA((n_dp + 1,)),
             pltpu.SemaphoreType.DMA((8 * n_dp,)),
             pltpu.SemaphoreType.DMA((n_label,)),
             pltpu.SemaphoreType.DMA((n_label,)),

time: 101 us -> 92.1 us (0.912)
  Pallas kernels: 89.9 us -> 81.3 us
    pallas_call x1, Pallas kernels: 89.9 us -> 81.3 us  [sparse_body(): pl.pallas_call(functools.partial(step_kernel, n_dp, n_label, beams.shape[...]
where the time goes in v2:
time: 92.1 us; the launch traced here: 91.8 us
  Pallas kernels  81.3 us (88%)
  local copies, waits for them, and re-layouts  6.73 us (7%)
  other arithmetic  3.14 us (3%)
    pallas_call x1, Pallas kernels, sparse_body(): pl.pallas_call(functools.partial(step_kernel, n_dp, n_label, beams.shape[...  81.3 us
    unnamed x4, local copies, waits for them, and re-layouts  6.68 us

profile of v2, /device:TPU:0, one launch (start us, length us, event | category | flops | bytes accessed | tf_op | source)
XLA Modules:
  0.0 91.8 jit_solution(8118533812815298697)
XLA Ops:
  0.6 0.0 copy-start
  0.6 0.7 add_select_fusion.1
  1.4 1.6 %select_reduce_fusion = s32[128,20]{0,1:T(8,128)S(1)} fusion(s32[256]{0:T(256)} %param.8, s32[128,20]{0,1:T(8,128)} %param.6), kind=kLoop, calls=%fused_computation | loop fusion | flops 1963520 | bytes 21504 | tf_op jit(solution)/shard_map/reduce_sum | solution.py:398
  3.1 0.0 copy-done
  3.1 0.7 pad_maximum_fusion.mine_ref
  3.9 81.3 %shard_map.68 = (f32[128,1024]{1,0:T(8,128)}, f32[8,128,1024]{2,1,0:T(8,128)}) custom-call(bf16[1088,128]{1,0:T(8,128)(2,1)} %pad_maximum_fusion.mine_ref, bf16[32,128,1024]{2,1,0:T(8,128)(2,1)} %bitcast.12), custom_call_target="tpu_custom_call" | custom-call | tf_op jit(solution)/shard_map/pallas_call | solution.py:423
  85.2 1.9 %copy.16 = f32[128,1024]{1,0:T(8,128)} copy(f32[128,1024]{1,0:T(8,128)} %get-tuple-element.10) | data formatting | bytes 1048576
  87.0 4.8 %copy.17 = f32[1024,1024]{1,0:T(8,128)} copy(f32[1024,1024]{1,0:T(8,128)} %bitcast.13) | data formatting | bytes 8388608
  (5 shorter events, 0.1 us)
Async XLA Ops:
  0.6 2.5 %copy-start = (bf16[128,1024]{1,0:T(8,128)(2,1)S(1)}, bf16[128,1024]{1,0:T(8,128)(2,1)}, u32[]{:S(2)}) copy-start(bf16[128,1024]{1,0:T(8,128)(2,1)} %param.5) | copy-start | bytes 786436

commit v3 on v2

--- a/solution.py
+++ b/solution.py
@@ -231,6 +231,17 @@
         base = planes[s] * n_label
         own, gx, gy, gd = base + l, base + xn, base + yn, base + diag
         sem = [send_sem.at[s * 8 + i] for i in range(8)]
+        if s == 1:
+            ux, uy, ud = (d * n_label + k for k in (xn, yn, diag))
+            return [
+                (ux, whole, sem[0], recv_sem.at[ux], (near, l)),
+                (uy, whole, sem[1], recv_sem.at[uy], (near, l)),
+                (own, whole, sem[2], recv_sem.at[own], (d, sib)),
+                (ud, whole, sem[3], recv_sem.at[ud], (near, l)),
+                (gx, whole, sem[4], recv_sem.at[gx], (d, sib)),
+                (gy, whole, sem[6], recv_sem.at[gy], (d, sib)),
+                (gd, whole, sem[7], recv_sem.at[gd], (d, sib)),
+            ]
         return [
             (own, whole, sem[0], recv_sem.at[own], (d, xn)),
             (own, whole, sem[1], recv_sem.at[own], (d, yn)),
@@ -253,23 +264,28 @@
         def _():
             z_copy(s).start()
 
-        for c in sends(s)[:3]:
+        for c in sends(s)[2 if s == 1 else 0:3]:
             copy(*c).start()
 
     def stage_b(s):
         gx, gy = planes[s] * n_label + xn, planes[s] * n_label + yn
         arrived(gx, whole, recv_sem.at[gx])
-        for c in sends(s)[3:5]:
+        for c in sends(s)[4 if s == 1 else 3:5]:
             copy(*c).start()
         arrived(gy, whole, recv_sem.at[gy])
-        for c in sends(s)[5:7]:
+        for c in sends(s)[5:6 if s == 1 else 7]:
             copy(*c).start()
 
     def stage_c(s):
         g = planes[s] * n_label + diag
-        arrived(g, first, recv_sem.at[g])
-        arrived(g, second, half_sem.at[planes[s]])
-        copy(*sends(s)[7]).start()
+        arrived(g, whole if s == 1 else first, recv_sem.at[g])
+        if s != 1:
+            arrived(g, second, half_sem.at[planes[s]])
+        copy(*sends(s)[-1]).start()
+
+    def send_near():
+        for i in (0, 1, 3):
+            copy(*sends(1)[i]).start()
 
     def stage_d(s):
         for j in (1, 3, 5, 7):
@@ -288,10 +304,10 @@
                 pick_ref[j, h * rows:(h + 1) * rows, :] = pick
 
     def signals(start, stop):
-        @pl.loop(start // 2, stop // 2)
+        @pl.loop(start // 4, stop // 4)
         def _(c2):
-            for u in range(2):
-                c = c2 * 2 + u
+            for u in range(4):
+                c = c2 * 4 + u
                 w = w_ref[c]
                 sig = signal_of(x_ref[c], off_ref[c], w, n_pos)
                 sig_ref[c] = sig
@@ -320,10 +336,9 @@
     stage_a(2)
     gather_own(6, 7, 1)
     stage_d(0)
-    stage_b(1)
     gather_own(1, 4, 2)
     stage_a(3)
-    stage_c(1)
+    send_near()
     gather_own(5, 8, 2)
     stage_b(2)
     load_w.wait()
@@ -331,8 +346,11 @@
     stage_c(2)
     stage_b(3)
     signals(quarter, 2 * quarter)
+    stage_b(1)
+    signals(2 * quarter, 3 * quarter)
     stage_c(3)
-    signals(2 * quarter, clus_dev)
+    stage_c(1)
+    signals(3 * quarter, clus_dev)
     for j in (7, 3, 5, 1):
         part_ref[j] = part_of(j).astype(jnp.bfloat16)
         grad_copy(j).start()
@@ -354,19 +372,19 @@
     for s in range(1, n_dp):
         stage_d(s)
 
-        @pl.loop(0, n_label // 2)
+        @pl.loop(0, n_label // 4)
         def _(i):
-            for u in range(2):
-                j = i * 2 + u
+            for u in range(4):
+                j = i * 4 + u
                 gather_chunk(
                     blk_ref, planes[s] * n_label + j, j, l * clus_dev + d * CHUNK, 0, beam,
                     x_ref, off_ref,
                 )
 
-        @pl.loop(0, CHUNK // 2)
+        @pl.loop(0, CHUNK // 4)
         def _(c2):
-            for u in range(2):
-                c = c2 * 2 + u
+            for u in range(4):
+                c = c2 * 4 + u
                 x = x_ref[c]
                 sig = signal_of(x, off_ref[c], w_ref[d * CHUNK + c], n_pos)
                 new_ref[c] = new_ref[c] - STEP_SIZE * tn_dot(sig, x)

time: 92.1 us -> 84 us (0.912)
  Pallas kernels: 81.3 us -> 73.2 us
    pallas_call x1, Pallas kernels: 81.3 us -> 73.2 us  [sparse_body(): pl.pallas_call(functools.partial(step_kernel, n_dp, n_label, beams.shape[...]
where the time goes in v3:
time: 84 us; the launch traced here: 83.8 us
  Pallas kernels  73.2 us (87%)
  local copies, waits for them, and re-layouts  6.73 us (8%)
  other arithmetic  3.14 us (4%)
    pallas_call x1, Pallas kernels, sparse_body(): pl.pallas_call(functools.partial(step_kernel, n_dp, n_label, beams.shape[...  73.2 us
    unnamed x4, local copies, waits for them, and re-layouts  6.68 us

profile of v3, /device:TPU:0, one launch (start us, length us, event | category | flops | bytes accessed | tf_op | source)
XLA Modules:
  0.0 83.8 jit_solution(1863745419415543681)
XLA Ops:
  0.6 0.0 copy-start
  0.6 0.7 add_select_fusion.1
  1.4 1.6 %select_reduce_fusion = s32[128,20]{0,1:T(8,128)S(1)} fusion(s32[256]{0:T(256)} %param.8, s32[128,20]{0,1:T(8,128)} %param.6), kind=kLoop, calls=%fused_computation | loop fusion | flops 1963520 | bytes 21504 | tf_op jit(solution)/shard_map/reduce_sum | solution.py:416
  3.1 0.0 copy-done
  3.1 0.7 pad_maximum_fusion.mine_ref
  3.9 73.2 %shard_map.68 = (f32[128,1024]{1,0:T(8,128)}, f32[8,128,1024]{2,1,0:T(8,128)}) custom-call(bf16[1088,128]{1,0:T(8,128)(2,1)} %pad_maximum_fusion.mine_ref, bf16[32,128,1024]{2,1,0:T(8,128)(2,1)} %bitcast.12), custom_call_target="tpu_custom_call" | custom-call | tf_op jit(solution)/shard_map/pallas_call | solution.py:441
  77.1 1.9 %copy.16 = f32[128,1024]{1,0:T(8,128)} copy(f32[128,1024]{1,0:T(8,128)} %get-tuple-element.10) | data formatting | bytes 1048576
  79.0 4.8 %copy.17 = f32[1024,1024]{1,0:T(8,128)} copy(f32[1024,1024]{1,0:T(8,128)} %bitcast.13) | data formatting | bytes 8388608
  (5 shorter events, 0.1 us)
Async XLA Ops:
  0.6 2.5 %copy-start = (bf16[128,1024]{1,0:T(8,128)(2,1)S(1)}, bf16[128,1024]{1,0:T(8,128)(2,1)}, u32[]{:S(2)}) copy-start(bf16[128,1024]{1,0:T(8,128)(2,1)} %param.5) | copy-start | bytes 786436

commit v4 on v3

--- a/solution.py
+++ b/solution.py
@@ -369,22 +369,22 @@
         at = d * CHUNK + c
         new_ref[c] = w_ref[at].astype(jnp.float32) - STEP_SIZE * tn_dot(sig_ref[at], x_ref[at])
 
-    for s in range(1, n_dp):
+    for s in (2, 3, 1):
         stage_d(s)
 
-        @pl.loop(0, n_label // 4)
+        @pl.loop(0, n_label // 8)
         def _(i):
-            for u in range(4):
-                j = i * 4 + u
+            for u in range(8):
+                j = i * 8 + u
                 gather_chunk(
                     blk_ref, planes[s] * n_label + j, j, l * clus_dev + d * CHUNK, 0, beam,
                     x_ref, off_ref,
                 )
 
-        @pl.loop(0, CHUNK // 4)
+        @pl.loop(0, CHUNK // 8)
         def _(c2):
-            for u in range(4):
-                c = c2 * 4 + u
+            for u in range(8):
+                c = c2 * 8 + u
                 x = x_ref[c]
                 sig = signal_of(x, off_ref[c], w_ref[d * CHUNK + c], n_pos)
                 new_ref[c] = new_ref[c] - STEP_SIZE * tn_dot(sig, x)

time: 84 us -> 81.1 us (0.965)
  Pallas kernels: 73.2 us -> 70.3 us
    pallas_call x1, Pallas kernels: 73.2 us -> 70.3 us  [sparse_body(): pl.pallas_call(functools.partial(step_kernel, n_dp, n_label, beams.shape[...]
where the time goes in v4:
time: 81.1 us; the launch traced here: 80.9 us
  Pallas kernels  70.3 us (87%)
  local copies, waits for them, and re-layouts  6.73 us (8%)
  other arithmetic  3.14 us (4%)
    pallas_call x1, Pallas kernels, sparse_body(): pl.pallas_call(functools.partial(step_kernel, n_dp, n_label, beams.shape[...  70.3 us
    unnamed x4, local copies, waits for them, and re-layouts  6.68 us
    reduce_sum x1, other arithmetic, make_block(): slot = jnp.sum(jnp.where(lookup, owner[None, None, :], 0), axis=2)  1.63 us

profile of v4, /device:TPU:0, one launch (start us, length us, event | category | flops | bytes accessed | tf_op | source)
XLA Modules:
  0.0 80.9 jit_solution(2640893801689732318)
XLA Ops:
  0.6 0.0 copy-start
  0.6 0.7 add_select_fusion.1
  1.4 1.6 %select_reduce_fusion = s32[128,20]{0,1:T(8,128)S(1)} fusion(s32[256]{0:T(256)} %param.8, s32[128,20]{0,1:T(8,128)} %param.6), kind=kLoop, calls=%fused_computation | loop fusion | flops 1963520 | bytes 21504 | tf_op jit(solution)/shard_map/reduce_sum | solution.py:416
  3.1 0.0 copy-done
  3.1 0.7 pad_maximum_fusion.mine_ref
  3.9 70.3 %shard_map.68 = (f32[128,1024]{1,0:T(8,128)}, f32[8,128,1024]{2,1,0:T(8,128)}) custom-call(bf16[1088,128]{1,0:T(8,128)(2,1)} %pad_maximum_fusion.mine_ref, bf16[32,128,1024]{2,1,0:T(8,128)(2,1)} %bitcast.12), custom_call_target="tpu_custom_call" | custom-call | tf_op jit(solution)/shard_map/pallas_call | solution.py:441
  74.2 1.9 %copy.16 = f32[128,1024]{1,0:T(8,128)} copy(f32[128,1024]{1,0:T(8,128)} %get-tuple-element.10) | data formatting | bytes 1048576
  76.1 4.8 %copy.17 = f32[1024,1024]{1,0:T(8,128)} copy(f32[1024,1024]{1,0:T(8,128)} %bitcast.13) | data formatting | bytes 8388608
  (5 shorter events, 0.1 us)
Async XLA Ops:
  0.6 2.5 %copy-start = (bf16[128,1024]{1,0:T(8,128)(2,1)S(1)}, bf16[128,1024]{1,0:T(8,128)(2,1)}, u32[]{:S(2)}) copy-start(bf16[128,1024]{1,0:T(8,128)(2,1)} %param.5) | copy-start | bytes 786436
